TPU v7x, 32 devices: a whole 2x2x4 slice. The times are simulated.
32 devices in a mesh: obs: 8 (over z, x), tile: 4 (over y, core).
Axes of the slice: x: 2, y: 2, z: 4, core: 2. Of those that a mesh axis runs over, the one named last changes fastest.
Arguments:
- jacobian: bfloat16 [2048, 65536], P(('obs', 'tile')), may hold values from -0.5 to 0.5
- obs_weight: float32 [2048], P(('obs', 'tile')), may hold values from 0.1 to 10
- block_order: int32 [512], replicated, may hold values from 0 to 511, each once
- tile_pairs: int32 [8, 64, 2], P('obs'), may hold values from 0 to 63, as said below
- tile_count: int32 [8], P('obs'), may hold values from 1 to 64, as said below
Outputs:
- hessian: float32 [512, 128, 128], P(('obs', 'tile'))
Inputs may be any that keep to these rules, and one draw needn't show every extreme that they name: `tile_pairs`: slot numbers within an owner's own 64 slots; the first tile_count[j] pairs of owner j are distinct. `tile_count`: some owner has 64 live tiles.
All inputs are finite; a program needn't handle non-finite values.
Results may differ from a plain program's by a relative error of at most 0.0015.
Values may be sent and summed in bfloat16 or wider, within the bound.
A program may use at most 256 MiB of HBM per device.

v0:
```python
import functools
import jax
import jax.numpy as jnp
from jax import lax
from jax.experimental import pallas as pl
from jax.experimental.pallas import tpu as pltpu
from jax.sharding import Mesh, PartitionSpec as P

BLOCK = 128
PARTS = 2


def order_kernel(slots, parts, per_part, order_ref, jac_ref, weight_ref, out_ref):
    dest, part = pl.program_id(0), pl.program_id(1)
    first = (part * per_part + dest) * slots
    weight = jnp.broadcast_to(weight_ref[...], (weight_ref.shape[0], BLOCK))

    def one(slot, carry):
        start = pl.multiple_of(order_ref[first + slot] * BLOCK, BLOCK)
        piece = jac_ref[:, pl.ds(start, BLOCK)].astype(jnp.float32) * weight
        out_ref[0, 0, slot] = piece.astype(jnp.bfloat16)
        return carry

    lax.fori_loop(0, slots, one, 0, unroll=8)


def order_columns(jacobian, root_weight, block_order, parts, per_part):
    rows, width = jacobian.shape
    slots = block_order.shape[0] // (parts * per_part)
    return pl.pallas_call(
        functools.partial(order_kernel, slots, parts, per_part),
        out_shape=jax.ShapeDtypeStruct((per_part, parts, slots, rows, BLOCK), jnp.bfloat16),
        grid_spec=pltpu.PrefetchScalarGridSpec(
            num_scalar_prefetch=1,
            grid=(per_part, parts),
            in_specs=[
                pl.BlockSpec((rows, width), lambda d, p, order: (0, 0)),
                pl.BlockSpec((rows, 1), lambda d, p, order: (0, 0)),
            ],
            out_specs=pl.BlockSpec((1, 1, slots, rows, BLOCK), lambda d, p, order: (d, p, 0, 0, 0)),
        ),
        compiler_params=pltpu.CompilerParams(vmem_limit_bytes=48 << 20),
    )(block_order, jacobian, root_weight)


def kernel(n, rows, quarter, own_list, far_list, sent_ref, out_ref,
           far_cols, own_cols, far_tiles, own_tiles, pair_in, side_in, part_in,
           far_ss, far_rs, own_ss, own_rs, pair_ss, pair_rs, side_ss, side_rs, part_ss, part_rs):
    part, me, t = lax.axis_index("part"), lax.axis_index("obs"), lax.axis_index("tile")
    hi, lo = t // 2, t % 2
    pair_peer = {"tile": hi * 2 + (1 - lo)}
    side_peer = {"tile": (1 - hi) * 2 + lo}
    part_peer = {"part": 1 - part}
    peers = [{"obs": (me + d) % n} for d in range(n)]
    mesh_id = pl.DeviceIdType.MESH

    barrier = pltpu.get_barrier_semaphore()
    for peer in peers[1:] + [pair_peer, side_peer, part_peer]:
        pl.semaphore_signal(barrier, inc=1, device_id=peer, device_id_type=mesh_id)

    def send(source, target, ss, rs, peer):
        return pltpu.make_async_remote_copy(
            src_ref=source, dst_ref=target, send_sem=ss, recv_sem=rs,
            device_id=peer, device_id_type=mesh_id)

    far_moves, own_moves = [None], [None]
    for d in range(1, n):
        dest = (me + d) % n
        place = pl.ds(d * rows, rows)
        far_moves.append(
            send(sent_ref.at[dest, 0], far_cols.at[:, place], far_ss.at[d], far_rs.at[d], peers[d]))
        own_moves.append(
            send(sent_ref.at[dest, 1], own_cols.at[:, place], own_ss.at[d], own_rs.at[d], peers[d]))
    far_kept = pltpu.make_async_copy(sent_ref.at[me, 0], far_cols.at[:, pl.ds(0, rows)], far_ss.at[0])
    own_kept = pltpu.make_async_copy(sent_ref.at[me, 1], own_cols.at[:, pl.ds(0, rows)], own_ss.at[0])
    pl.semaphore_wait(barrier, n + 2)
    for d in range(1, n):
        far_moves[d].start()
    far_kept.start()
    own_kept.start()
    for d in range(1, n):
        far_moves[d].wait_send()
        own_moves[d].start()
    far_kept.wait()
    own_kept.wait()

    half = quarter // 2
    halves = [pl.ds(0, half), pl.ds(half, half)]

    def products(listed, columns, tiles, q, place, first, size):
        def one(i, carry):
            tile = q * quarter + first + i
            left = columns[listed[2 * tile]]
            right = columns[listed[2 * tile + 1]]
            tiles[place, first + i] = lax.dot_general(
                left, right, (((0,), (0,)), ((), ())), preferred_element_type=jnp.float32)
            return carry

        lax.fori_loop(0, size, one, 0, unroll=4)

    def reduce(phase, listed, columns, tiles):
        near, side = [], []
        for i, part_half in enumerate(halves):
            near.append(send(tiles.at[0, part_half], pair_in.at[phase, 0, part_half],
                             pair_ss.at[phase, i], pair_rs.at[phase, i], pair_peer))
            side.append(send(tiles.at[1, part_half], side_in.at[phase, part_half],
                             side_ss.at[phase, i], side_rs.at[phase, i], side_peer))
        near.append(send(tiles.at[2], pair_in.at[phase, 1],
                         pair_ss.at[phase, 2], pair_rs.at[phase, 2], pair_peer))
        for i, part_half in enumerate(halves):
            products(listed, columns, tiles, (1 - hi) * 2 + (1 - lo), 0, i * half, half)
            near[i].start()
            products(listed, columns, tiles, (1 - hi) * 2 + lo, 1, i * half, half)
            near[i].wait_recv()
            tiles[1, part_half] = tiles[1, part_half] + pair_in[phase, 0, part_half]
            side[i].start()
        products(listed, columns, tiles, hi * 2 + (1 - lo), 2, 0, quarter)
        near[2].start()
        products(listed, columns, tiles, hi * 2 + lo, 3, 0, quarter)
        near[2].wait_recv()
        tiles[3] = tiles[3] + pair_in[phase, 1]
        return near, side

    for d in range(1, n):
        far_moves[d].wait_recv()
    far_near, far_side = reduce(0, far_list, far_cols, far_tiles)
    for move in far_side:
        move.wait_recv()
    far_tiles[3] = far_tiles[3] + side_in[0]
    across = send(far_tiles.at[3], part_in, part_ss, part_rs, part_peer)
    across.start()
    for d in range(1, n):
        own_moves[d].wait_recv()
    own_near, own_side = reduce(1, own_list, own_cols, own_tiles)
    across.wait_recv()
    own_tiles[3] = own_tiles[3] + part_in[...]
    for move in own_side:
        move.wait_recv()
    out_ref[...] = own_tiles[3] + side_in[1]
    for d in range(1, n):
        own_moves[d].wait_send()
    for move in far_near + own_near + far_side + own_side + [across]:
        move.wait_send()


def body(n, jacobian, obs_weight, block_order, tile_pairs, tile_count):
    rows, width = jacobian.shape
    slots = block_order.shape[0] // (PARTS * n)
    tiles = tile_pairs.shape[1]
    quarter = tiles // 4
    root_weight = jnp.sqrt(obs_weight)[:, None]
    listed = tile_pairs.reshape(-1)
    far_listed = lax.ppermute(listed, "part", [(0, 1), (1, 0)])
    smem = pl.BlockSpec(memory_space=pltpu.SMEM)
    vmem = pl.BlockSpec(memory_space=pltpu.VMEM)
    dma = pltpu.SemaphoreType.DMA
    here = lax.axis_index("part")
    orders = block_order.reshape(PARTS, -1)
    orders = jnp.where(here == 0, orders[::-1], orders).reshape(-1)
    sent = order_columns(jacobian, root_weight, orders, PARTS, n)
    held_cols = pltpu.VMEM((slots, n * rows, BLOCK), jnp.bfloat16)
    group = (quarter, BLOCK, BLOCK)
    held = pl.pallas_call(
        functools.partial(kernel, n, rows, quarter),
        out_shape=jax.ShapeDtypeStruct(group, jnp.float32),
        in_specs=[smem, smem, pl.BlockSpec(memory_space=pl.ANY)],
        out_specs=vmem,
        scratch_shapes=[
            held_cols,
            held_cols,
            pltpu.VMEM((4,) + group, jnp.float32),
            pltpu.VMEM((4,) + group, jnp.float32),
            pltpu.VMEM((2, 2) + group, jnp.float32),
            pltpu.VMEM((2,) + group, jnp.float32),
            pltpu.VMEM(group, jnp.float32),
            dma((n,)), dma((n,)), dma((n,)), dma((n,)),
            dma((2, 3)), dma((2, 3)), dma((2, 2)), dma((2, 2)), dma, dma,
        ],
        compiler_params=pltpu.CompilerParams(
            collective_id=0, has_side_effects=True, vmem_limit_bytes=56 << 20),
    )(listed, far_listed, sent)
    ids = lax.axis_index("tile") * quarter + jnp.arange(quarter, dtype=jnp.int32)
    return jnp.where((ids < tile_count)[:, None, None], held, 0.0)


def solution(mesh):
    owners, tile_size = mesh.devices.shape
    n = owners // PARTS
    split_mesh = Mesh(mesh.devices.reshape(PARTS, n, tile_size), ("part", "obs", "tile"))
    every = ("part", "obs", "tile")
    return jax.shard_map(
        functools.partial(body, n),
        mesh=split_mesh,
        in_specs=(P(every, None), P(every), P(), P(("part", "obs"), None, None), P(("part", "obs"))),
        out_specs=P(every, None, None),
        check_vma=False,
    )
```

profile of v0, /device:TPU:3, one launch (start us, length us, event | category | flops | bytes accessed | tf_op | source)
XLA Modules:
  0.0 157.9 jit_solution(16610217447163582843)
XLA Ops:
  0.0 0.8 copy.8
  0.8 0.1 reshape.14.own_list
  0.9 0.0 copy-start
  0.9 2.4 %collective-permute-start = (s32[128]{0:T(128)S(1)}, s32[128]{0:T(128)S(1)}, u32[]{:S(2)}, u32[]{:S(2)}) collective-permute-start(s32[128]{0:T(128)S(1)} %reshape.14.own_list), channel_id=1, source_target_pairs={{0,16},{16,0},{1,17},{17,1},{2,18},{18,2},{3,19},{19,3},{4,20},{20... | collective-permute-start | bytes 1544 | tf_op jit(solution)/shard_map/ppermute | solution.py:153
  3.9 0.7 sqrt_bitcast_fusion
  4.6 0.7 reshape.15
  5.3 0.1 rev.3
  5.4 0.1 copy.9.weight_ref
  5.5 10.1 %shard_map.55.sent_ref = bf16[4,2,64,64,128]{4,3,2,1,0:T(8,128)(2,1)} custom-call(s32[512]{0:T(512)S(1)} %bitcast.7, bf16[64,65536]{1,0:T(8,128)(2,1)} %jac_ref.1, f32[64,1]{1,0:T(8,128)S(1)} %copy.9.weight_ref), custom_call_target="tpu_custom_call" | custom-call | tf_op jit(solution)/shard_map/pallas_call | solution.py:30
  15.6 0.0 copy-done
  15.6 0.0 collective-permute-done.far_list
  15.6 0.0 copy-start.1
  15.6 0.6 copy-done.1
  16.1 139.4 %shard_map.56 = f32[16,128,128]{2,1,0:T(8,128)} custom-call(s32[128]{0:T(128)} %copy-done, s32[128]{0:T(128)} %copy-done.1, bf16[4,2,64,64,128]{4,3,2,1,0:T(8,128)(2,1)} %shard_map.55.sent_ref), custom_call_target="tpu_custom_call" | custom-call | tf_op jit(solution)/shard_map/pallas_call | solution.py:163
  155.6 2.3 %broadcast_select_fusion = f32[16,128,128]{2,1,0:T(8,128)} fusion(f32[16,128,128]{2,1,0:T(8,128)} %shard_map.56, pred[16]{0:T(512)(128)(4,1)S(1)} %add_compare_fusion), kind=kLoop, calls=%fused_computation | loop fusion | flops 262144 | bytes 2097168 | tf_op jit(solution)/shard_map/jit(_where)/select_n | solution.py:183
  (3 shorter events, 0.0 us)
Async XLA Ops:
  0.9 14.7 %copy-start = (s32[128]{0:T(128)}, s32[128]{0:T(128)S(1)}, u32[]{:S(2)}) copy-start(s32[128]{0:T(128)S(1)} %reshape.14.own_list) | copy-start | bytes 1540
  0.9 14.6 %collective-permute-start = (s32[128]{0:T(128)S(1)}, s32[128]{0:T(128)S(1)}, u32[]{:S(2)}, u32[]{:S(2)}) collective-permute-start(s32[128]{0:T(128)S(1)} %reshape.14.own_list), channel_id=1, source_target_pairs={{0,16},{16,0},{1,17},{17,1},{2,18},{18,2},{3,19},{19,3},{4,20},{20... | collective-permute-start | bytes 1544 | tf_op jit(solution)/shard_map/ppermute | solution.py:153
  15.6 0.6 copy-start.1
where the time goes:
time: 158 us
  Pallas kernels  149 us (94%)
  local copies, waits for them, and re-layouts  3 us (2%)
  starting transfers between devices  2.37 us (2%)
  other arithmetic  2.35 us (1%)
    pallas_call x1, Pallas kernels, body(): pl.pallas_call(functools.partial(kernel, n, rows, quarter), out_shape=jax...  139 us
    pallas_call x1, Pallas kernels, order_columns(): pl.pallas_call(functools.partial(order_kernel, slots, parts, per_part), o...  10.1 us
  transfers between devices with their start and end apart: 1, of which 0 were waited for; matrix products, arithmetic and copies ran while one was open for 1% of the time, Pallas kernels for 6%

commit v1 on v0

--- a/solution.py
+++ b/solution.py
@@ -11,17 +11,19 @@
 
 
 def order_kernel(slots, parts, per_part, order_ref, jac_ref, weight_ref, out_ref):
-    dest, part = pl.program_id(0), pl.program_id(1)
-    first = (part * per_part + dest) * slots
+    dest = pl.program_id(0)
     weight = jnp.broadcast_to(weight_ref[...], (weight_ref.shape[0], BLOCK))
 
-    def one(slot, carry):
-        start = pl.multiple_of(order_ref[first + slot] * BLOCK, BLOCK)
-        piece = jac_ref[:, pl.ds(start, BLOCK)].astype(jnp.float32) * weight
-        out_ref[0, 0, slot] = piece.astype(jnp.bfloat16)
-        return carry
-
-    lax.fori_loop(0, slots, one, 0, unroll=8)
+    for part in range(parts):
+        first = (part * per_part + dest) * slots
+
+        def one(slot, carry, part=part, first=first):
+            start = pl.multiple_of(order_ref[first + slot] * BLOCK, BLOCK)
+            piece = jac_ref[:, pl.ds(start, BLOCK)].astype(jnp.float32) * weight
+            out_ref[0, part, slot] = piece.astype(jnp.bfloat16)
+            return carry
+
+        lax.fori_loop(0, slots, one, 0, unroll=8)
 
 
 def order_columns(jacobian, root_weight, block_order, parts, per_part):
@@ -32,20 +34,20 @@
         out_shape=jax.ShapeDtypeStruct((per_part, parts, slots, rows, BLOCK), jnp.bfloat16),
         grid_spec=pltpu.PrefetchScalarGridSpec(
             num_scalar_prefetch=1,
-            grid=(per_part, parts),
+            grid=(per_part,),
             in_specs=[
-                pl.BlockSpec((rows, width), lambda d, p, order: (0, 0)),
-                pl.BlockSpec((rows, 1), lambda d, p, order: (0, 0)),
+                pl.BlockSpec((rows, width), lambda d, order: (0, 0)),
+                pl.BlockSpec((rows, 1), lambda d, order: (0, 0)),
             ],
-            out_specs=pl.BlockSpec((1, 1, slots, rows, BLOCK), lambda d, p, order: (d, p, 0, 0, 0)),
+            out_specs=pl.BlockSpec((1, parts, slots, rows, BLOCK), lambda d, order: (d, 0, 0, 0, 0)),
         ),
         compiler_params=pltpu.CompilerParams(vmem_limit_bytes=48 << 20),
     )(block_order, jacobian, root_weight)
 
 
-def kernel(n, rows, quarter, own_list, far_list, sent_ref, out_ref,
-           far_cols, own_cols, far_tiles, own_tiles, pair_in, side_in, part_in,
-           far_ss, far_rs, own_ss, own_rs, pair_ss, pair_rs, side_ss, side_rs, part_ss, part_rs):
+def kernel(n, rows, quarter, own_list, own_row, sent_ref, out_ref,
+           far_row, far_list, far_cols, own_cols, far_tiles, own_tiles, pair_in, side_in, part_in,
+           far_ss, far_rs, own_ss, own_rs, pair_ss, pair_rs, side_ss, side_rs, part_ss, part_rs, list_ss, list_rs):
     part, me, t = lax.axis_index("part"), lax.axis_index("obs"), lax.axis_index("tile")
     hi, lo = t // 2, t % 2
     pair_peer = {"tile": hi * 2 + (1 - lo)}
@@ -76,6 +78,8 @@
     pl.semaphore_wait(barrier, n + 2)
     for d in range(1, n):
         far_moves[d].start()
+    list_move = send(own_row, far_row, list_ss.at[0], list_rs, part_peer)
+    list_move.start()
     far_kept.start()
     own_kept.start()
     for d in range(1, n):
@@ -83,6 +87,10 @@
         own_moves[d].start()
     far_kept.wait()
     own_kept.wait()
+    list_move.wait()
+    list_kept = pltpu.make_async_copy(far_row, far_list, list_ss.at[1])
+    list_kept.start()
+    list_kept.wait()
 
     half = quarter // 2
     halves = [pl.ds(0, half), pl.ds(half, half)]
@@ -90,8 +98,8 @@
     def products(listed, columns, tiles, q, place, first, size):
         def one(i, carry):
             tile = q * quarter + first + i
-            left = columns[listed[2 * tile]]
-            right = columns[listed[2 * tile + 1]]
+            left = columns[listed[0, 2 * tile]]
+            right = columns[listed[0, 2 * tile + 1]]
             tiles[place, first + i] = lax.dot_general(
                 left, right, (((0,), (0,)), ((), ())), preferred_element_type=jnp.float32)
             return carry
@@ -124,22 +132,23 @@
     for d in range(1, n):
         far_moves[d].wait_recv()
     far_near, far_side = reduce(0, far_list, far_cols, far_tiles)
-    for move in far_side:
-        move.wait_recv()
-    far_tiles[3] = far_tiles[3] + side_in[0]
-    across = send(far_tiles.at[3], part_in, part_ss, part_rs, part_peer)
-    across.start()
+    across = []
+    for i, part_half in enumerate(halves):
+        far_side[i].wait_recv()
+        far_tiles[3, part_half] = far_tiles[3, part_half] + side_in[0, part_half]
+        across.append(send(far_tiles.at[3, part_half], part_in.at[part_half],
+                           part_ss.at[i], part_rs.at[i], part_peer))
+        across[i].start()
     for d in range(1, n):
         own_moves[d].wait_recv()
     own_near, own_side = reduce(1, own_list, own_cols, own_tiles)
-    across.wait_recv()
-    own_tiles[3] = own_tiles[3] + part_in[...]
-    for move in own_side:
-        move.wait_recv()
-    out_ref[...] = own_tiles[3] + side_in[1]
+    for i, part_half in enumerate(halves):
+        across[i].wait_recv()
+        own_side[i].wait_recv()
+        out_ref[part_half] = (own_tiles[3, part_half] + part_in[part_half]) + side_in[1, part_half]
     for d in range(1, n):
         own_moves[d].wait_send()
-    for move in far_near + own_near + far_side + own_side + [across]:
+    for move in far_near + own_near + far_side + own_side + across:
         move.wait_send()
 
 
@@ -149,8 +158,7 @@
     tiles = tile_pairs.shape[1]
     quarter = tiles // 4
     root_weight = jnp.sqrt(obs_weight)[:, None]
-    listed = tile_pairs.reshape(-1)
-    far_listed = lax.ppermute(listed, "part", [(0, 1), (1, 0)])
+    listed = tile_pairs.reshape(1, -1)
     smem = pl.BlockSpec(memory_space=pltpu.SMEM)
     vmem = pl.BlockSpec(memory_space=pltpu.VMEM)
     dma = pltpu.SemaphoreType.DMA
@@ -163,9 +171,11 @@
     held = pl.pallas_call(
         functools.partial(kernel, n, rows, quarter),
         out_shape=jax.ShapeDtypeStruct(group, jnp.float32),
-        in_specs=[smem, smem, pl.BlockSpec(memory_space=pl.ANY)],
+        in_specs=[smem, vmem, pl.BlockSpec(memory_space=pl.ANY)],
         out_specs=vmem,
         scratch_shapes=[
+            pltpu.VMEM(listed.shape, jnp.int32),
+            pltpu.SMEM(listed.shape, jnp.int32),
             held_cols,
             held_cols,
             pltpu.VMEM((4,) + group, jnp.float32),
@@ -174,11 +184,11 @@
             pltpu.VMEM((2,) + group, jnp.float32),
             pltpu.VMEM(group, jnp.float32),
             dma((n,)), dma((n,)), dma((n,)), dma((n,)),
-            dma((2, 3)), dma((2, 3)), dma((2, 2)), dma((2, 2)), dma, dma,
+            dma((2, 3)), dma((2, 3)), dma((2, 2)), dma((2, 2)), dma((2,)), dma((2,)), dma((2,)), dma,
         ],
         compiler_params=pltpu.CompilerParams(
             collective_id=0, has_side_effects=True, vmem_limit_bytes=56 << 20),
-    )(listed, far_listed, sent)
+    )(listed, listed, sent)
     ids = lax.axis_index("tile") * quarter + jnp.arange(quarter, dtype=jnp.int32)
     return jnp.where((ids < tile_count)[:, None, None], held, 0.0)
 

time: 158 us -> 161 us (1.019)
  Pallas kernels: 149 us -> 155 us
  starting transfers between devices: 2.37 us -> 0 us
    pallas_call x1, Pallas kernels: 139 us -> 146 us  [body(): pl.pallas_call(functools.partial(kernel, n, rows, quarter), out_shape=jax...]
    ppermute x1 -> x0, starting transfers between devices: 2.37 us -> none  [body(): far_listed = lax.ppermute(listed, 'part', [(0, 1), (1, 0)])]
  transfers between devices with their start and end apart: 1 -> 0, of which waited for: 0 -> 0; matrix products, arithmetic and copies ran while one was open for 1% -> 0% of each run, Pallas kernels for 6% -> 0%
where the time goes in v1:
time: 161 us
  Pallas kernels  155 us (96%)
  local copies, waits for them, and re-layouts  2.93 us (2%)
  other arithmetic  2.35 us (1%)
    pallas_call x1, Pallas kernels, body(): pl.pallas_call(functools.partial(kernel, n, rows, quarter), out_shape=jax...  146 us
    pallas_call x1, Pallas kernels, order_columns(): pl.pallas_call(functools.partial(order_kernel, slots, parts, per_part), o...  8.97 us

profile of v1, /device:TPU:3, one launch (start us, length us, event | category | flops | bytes accessed | tf_op | source)
XLA Modules:
  0.0 161.2 jit_solution(8297414180715031453)
XLA Ops:
  0.7 0.7 sqrt_bitcast_fusion
  1.3 0.7 reshape.15
  2.0 0.1 rev.3
  2.1 0.1 copy.9.weight_ref
  2.2 0.8 copy.8
  3.0 0.7 reshape.14.own_list.own_row
  3.6 9.0 %shard_map.55.sent_ref = bf16[4,2,64,64,128]{4,3,2,1,0:T(8,128)(2,1)} custom-call(s32[512]{0:T(512)S(1)} %bitcast.7, bf16[64,65536]{1,0:T(8,128)(2,1)} %jac_ref.1, f32[64,1]{1,0:T(8,128)S(1)} %copy.9.weight_ref), custom_call_target="tpu_custom_call" | custom-call | tf_op jit(solution)/shard_map/pallas_call | solution.py:32
  12.6 146.2 %shard_map.56 = f32[16,128,128]{2,1,0:T(8,128)} custom-call(s32[1,128]{1,0:T(1,128)} %reshape.14.own_list.own_row, s32[1,128]{1,0:T(1,128)} %reshape.14.own_list.own_row, bf16[4,2,64,64,128]{4,3,2,1,0:T(8,128)(2,1)} %shard_map.55.sent_ref), custom_call_target="tpu_custom_call" | custom-call | tf_op jit(solution)/shard_map/pallas_call | solution.py:171
  158.8 2.3 %broadcast_select_fusion = f32[16,128,128]{2,1,0:T(8,128)} fusion(f32[16,128,128]{2,1,0:T(8,128)} %shard_map.56, pred[16]{0:T(512)(128)(4,1)S(1)} %add_compare_fusion), kind=kLoop, calls=%fused_computation | loop fusion | flops 262144 | bytes 2097168 | tf_op jit(solution)/shard_map/jit(_where)/select_n | solution.py:193
  (3 shorter events, 0.0 us)

commit v2 on v1

--- a/solution.py
+++ b/solution.py
@@ -45,6 +45,14 @@
     )(block_order, jacobian, root_weight)
 
 
+def partner(n, me, d):
+    other, bit = 0, 1
+    while bit < n:
+        other = other + (me // bit + d // bit) % 2 * bit
+        bit *= 2
+    return other
+
+
 def kernel(n, rows, quarter, own_list, own_row, sent_ref, out_ref,
            far_row, far_list, far_cols, own_cols, far_tiles, own_tiles, pair_in, side_in, part_in,
            far_ss, far_rs, own_ss, own_rs, pair_ss, pair_rs, side_ss, side_rs, part_ss, part_rs, list_ss, list_rs):
@@ -53,7 +61,7 @@
     pair_peer = {"tile": hi * 2 + (1 - lo)}
     side_peer = {"tile": (1 - hi) * 2 + lo}
     part_peer = {"part": 1 - part}
-    peers = [{"obs": (me + d) % n} for d in range(n)]
+    peers = [{"obs": partner(n, me, d)} for d in range(n)]
     mesh_id = pl.DeviceIdType.MESH
 
     barrier = pltpu.get_barrier_semaphore()
@@ -67,7 +75,7 @@
 
     far_moves, own_moves = [None], [None]
     for d in range(1, n):
-        dest = (me + d) % n
+        dest = partner(n, me, d)
         place = pl.ds(d * rows, rows)
         far_moves.append(
             send(sent_ref.at[dest, 0], far_cols.at[:, place], far_ss.at[d], far_rs.at[d], peers[d]))
@@ -76,13 +84,13 @@
     far_kept = pltpu.make_async_copy(sent_ref.at[me, 0], far_cols.at[:, pl.ds(0, rows)], far_ss.at[0])
     own_kept = pltpu.make_async_copy(sent_ref.at[me, 1], own_cols.at[:, pl.ds(0, rows)], own_ss.at[0])
     pl.semaphore_wait(barrier, n + 2)
-    for d in range(1, n):
+    for d in reversed(range(1, n)):
         far_moves[d].start()
     list_move = send(own_row, far_row, list_ss.at[0], list_rs, part_peer)
     list_move.start()
     far_kept.start()
     own_kept.start()
-    for d in range(1, n):
+    for d in reversed(range(1, n)):
         far_moves[d].wait_send()
         own_moves[d].start()
     far_kept.wait()
@@ -132,23 +140,21 @@
     for d in range(1, n):
         far_moves[d].wait_recv()
     far_near, far_side = reduce(0, far_list, far_cols, far_tiles)
-    across = []
-    for i, part_half in enumerate(halves):
-        far_side[i].wait_recv()
-        far_tiles[3, part_half] = far_tiles[3, part_half] + side_in[0, part_half]
-        across.append(send(far_tiles.at[3, part_half], part_in.at[part_half],
-                           part_ss.at[i], part_rs.at[i], part_peer))
-        across[i].start()
+    for move in far_side:
+        move.wait_recv()
+    far_tiles[3] = far_tiles[3] + side_in[0]
+    across = send(far_tiles.at[3], part_in, part_ss, part_rs, part_peer)
+    across.start()
     for d in range(1, n):
         own_moves[d].wait_recv()
     own_near, own_side = reduce(1, own_list, own_cols, own_tiles)
+    across.wait_recv()
     for i, part_half in enumerate(halves):
-        across[i].wait_recv()
         own_side[i].wait_recv()
         out_ref[part_half] = (own_tiles[3, part_half] + part_in[part_half]) + side_in[1, part_half]
     for d in range(1, n):
         own_moves[d].wait_send()
-    for move in far_near + own_near + far_side + own_side + across:
+    for move in far_near + own_near + far_side + own_side + [across]:
         move.wait_send()
 
 
@@ -184,7 +190,7 @@
             pltpu.VMEM((2,) + group, jnp.float32),
             pltpu.VMEM(group, jnp.float32),
             dma((n,)), dma((n,)), dma((n,)), dma((n,)),
-            dma((2, 3)), dma((2, 3)), dma((2, 2)), dma((2, 2)), dma((2,)), dma((2,)), dma((2,)), dma,
+            dma((2, 3)), dma((2, 3)), dma((2, 2)), dma((2, 2)), dma, dma, dma((2,)), dma,
         ],
         compiler_params=pltpu.CompilerParams(
             collective_id=0, has_side_effects=True, vmem_limit_bytes=56 << 20),
@@ -196,6 +202,7 @@
 def solution(mesh):
     owners, tile_size = mesh.devices.shape
     n = owners // PARTS
+    assert n & (n - 1) == 0 and tile_size == 4
     split_mesh = Mesh(mesh.devices.reshape(PARTS, n, tile_size), ("part", "obs", "tile"))
     every = ("part", "obs", "tile")
     return jax.shard_map(

time: 161 us -> 156 us (0.969); the launches traced: 161 us -> 154 us
  Pallas kernels: 155 us -> 148 us
    pallas_call x1, Pallas kernels: 146 us -> 139 us  [body(): pl.pallas_call(functools.partial(kernel, n, rows, quarter), out_shape=jax...]
where the time goes in v2:
time: 156 us; the launch traced here: 154 us
  Pallas kernels  148 us (95%)
  local copies, waits for them, and re-layouts  2.93 us (2%)
  other arithmetic  2.35 us (2%)
    pallas_call x1, Pallas kernels, body(): pl.pallas_call(functools.partial(kernel, n, rows, quarter), out_shape=jax...  139 us
    pallas_call x1, Pallas kernels, order_columns(): pl.pallas_call(functools.partial(order_kernel, slots, parts, per_part), o...  8.97 us

profile of v2, /device:TPU:3, one launch (start us, length us, event | category | flops | bytes accessed | tf_op | source)
XLA Modules:
  0.0 154.3 jit_solution(5857953458266920847)
XLA Ops:
  0.7 0.7 sqrt_bitcast_fusion
  1.3 0.7 reshape.15
  2.0 0.1 rev.3
  2.1 0.1 copy.9.weight_ref
  2.2 0.8 copy.8
  3.0 0.7 reshape.14.own_list.own_row
  3.6 9.0 %shard_map.55.sent_ref = bf16[4,2,64,64,128]{4,3,2,1,0:T(8,128)(2,1)} custom-call(s32[512]{0:T(512)S(1)} %bitcast.7, bf16[64,65536]{1,0:T(8,128)(2,1)} %jac_ref.1, f32[64,1]{1,0:T(8,128)S(1)} %copy.9.weight_ref), custom_call_target="tpu_custom_call" | custom-call | tf_op jit(solution)/shard_map/pallas_call | solution.py:32
  12.6 139.4 %shard_map.56 = f32[16,128,128]{2,1,0:T(8,128)} custom-call(s32[1,128]{1,0:T(1,128)} %reshape.14.own_list.own_row, s32[1,128]{1,0:T(1,128)} %reshape.14.own_list.own_row, bf16[4,2,64,64,128]{4,3,2,1,0:T(8,128)(2,1)} %shard_map.55.sent_ref), custom_call_target="tpu_custom_call" | custom-call | tf_op jit(solution)/shard_map/pallas_call | solution.py:177
  152.0 2.3 %broadcast_select_fusion = f32[16,128,128]{2,1,0:T(8,128)} fusion(f32[16,128,128]{2,1,0:T(8,128)} %shard_map.56, pred[16]{0:T(512)(128)(4,1)S(1)} %add_compare_fusion), kind=kLoop, calls=%fused_computation | loop fusion | flops 262144 | bytes 2097168 | tf_op jit(solution)/shard_map/jit(_where)/select_n | solution.py:199
  (3 shorter events, 0.0 us)

commit v3 on v2

--- a/solution.py
+++ b/solution.py
@@ -143,18 +143,22 @@
     for move in far_side:
         move.wait_recv()
     far_tiles[3] = far_tiles[3] + side_in[0]
-    across = send(far_tiles.at[3], part_in, part_ss, part_rs, part_peer)
-    across.start()
+    early = quarter * 3 // 8
+    across = [send(far_tiles.at[3, cut], part_in.at[cut], part_ss.at[i], part_rs.at[i], part_peer)
+              for i, cut in enumerate([pl.ds(0, early), pl.ds(early, quarter - early)])]
+    across[0].start()
     for d in range(1, n):
         own_moves[d].wait_recv()
+    across[1].start()
     own_near, own_side = reduce(1, own_list, own_cols, own_tiles)
-    across.wait_recv()
+    for move in across:
+        move.wait_recv()
     for i, part_half in enumerate(halves):
         own_side[i].wait_recv()
         out_ref[part_half] = (own_tiles[3, part_half] + part_in[part_half]) + side_in[1, part_half]
     for d in range(1, n):
         own_moves[d].wait_send()
-    for move in far_near + own_near + far_side + own_side + [across]:
+    for move in far_near + own_near + far_side + own_side + across:
         move.wait_send()
 
 
@@ -190,7 +194,7 @@
             pltpu.VMEM((2,) + group, jnp.float32),
             pltpu.VMEM(group, jnp.float32),
             dma((n,)), dma((n,)), dma((n,)), dma((n,)),
-            dma((2, 3)), dma((2, 3)), dma((2, 2)), dma((2, 2)), dma, dma, dma((2,)), dma,
+            dma((2, 3)), dma((2, 3)), dma((2, 2)), dma((2, 2)), dma((2,)), dma((2,)), dma((2,)), dma,
         ],
         compiler_params=pltpu.CompilerParams(
             collective_id=0, has_side_effects=True, vmem_limit_bytes=56 << 20),

time: 156 us -> 151 us (0.968)
  Pallas kernels: 148 us -> 144 us
    pallas_call x1, Pallas kernels: 139 us -> 135 us  [body(): pl.pallas_call(functools.partial(kernel, n, rows, quarter), out_shape=jax...]
where the time goes in v3:
time: 151 us; the launch traced here: 150 us
  Pallas kernels  144 us (95%)
  local copies, waits for them, and re-layouts  2.93 us (2%)
  other arithmetic  2.35 us (2%)
    pallas_call x1, Pallas kernels, body(): pl.pallas_call(functools.partial(kernel, n, rows, quarter), out_shape=jax...  135 us
    pallas_call x1, Pallas kernels, order_columns(): pl.pallas_call(functools.partial(order_kernel, slots, parts, per_part), o...  8.97 us

profile of v3, /device:TPU:3, one launch (start us, length us, event | category | flops | bytes accessed | tf_op | source)
XLA Modules:
  0.0 149.8 jit_solution(4810039335979178378)
XLA Ops:
  0.7 0.7 sqrt_bitcast_fusion
  1.3 0.7 reshape.15
  2.0 0.1 rev.3
  2.1 0.1 copy.9.weight_ref
  2.2 0.8 copy.8
  3.0 0.7 reshape.14.own_list.own_row
  3.6 9.0 %shard_map.55.sent_ref = bf16[4,2,64,64,128]{4,3,2,1,0:T(8,128)(2,1)} custom-call(s32[512]{0:T(512)S(1)} %bitcast.7, bf16[64,65536]{1,0:T(8,128)(2,1)} %jac_ref.1, f32[64,1]{1,0:T(8,128)S(1)} %copy.9.weight_ref), custom_call_target="tpu_custom_call" | custom-call | tf_op jit(solution)/shard_map/pallas_call | solution.py:32
  12.6 134.8 %shard_map.56 = f32[16,128,128]{2,1,0:T(8,128)} custom-call(s32[1,128]{1,0:T(1,128)} %reshape.14.own_list.own_row, s32[1,128]{1,0:T(1,128)} %reshape.14.own_list.own_row, bf16[4,2,64,64,128]{4,3,2,1,0:T(8,128)(2,1)} %shard_map.55.sent_ref), custom_call_target="tpu_custom_call" | custom-call | tf_op jit(solution)/shard_map/pallas_call | solution.py:181
  147.4 2.3 %broadcast_select_fusion = f32[16,128,128]{2,1,0:T(8,128)} fusion(f32[16,128,128]{2,1,0:T(8,128)} %shard_map.56, pred[16]{0:T(512)(128)(4,1)S(1)} %add_compare_fusion), kind=kLoop, calls=%fused_computation | loop fusion | flops 262144 | bytes 2097168 | tf_op jit(solution)/shard_map/jit(_where)/select_n | solution.py:203
  (3 shorter events, 0.0 us)

commit v4 on v3

--- a/solution.py
+++ b/solution.py
@@ -14,8 +14,9 @@
     dest = pl.program_id(0)
     weight = jnp.broadcast_to(weight_ref[...], (weight_ref.shape[0], BLOCK))
 
-    for part in range(parts):
-        first = (part * per_part + dest) * slots
+    here = lax.axis_index("part")
+    for part, owner_part in enumerate((1 - here, here)):
+        first = (owner_part * per_part + dest) * slots
 
         def one(slot, carry, part=part, first=first):
             start = pl.multiple_of(order_ref[first + slot] * BLOCK, BLOCK)
@@ -112,7 +113,7 @@
                 left, right, (((0,), (0,)), ((), ())), preferred_element_type=jnp.float32)
             return carry
 
-        lax.fori_loop(0, size, one, 0, unroll=4)
+        lax.fori_loop(0, size, one, 0, unroll=8)
 
     def reduce(phase, listed, columns, tiles):
         near, side = [], []
@@ -143,7 +144,7 @@
     for move in far_side:
         move.wait_recv()
     far_tiles[3] = far_tiles[3] + side_in[0]
-    early = quarter * 3 // 8
+    early = quarter // 2
     across = [send(far_tiles.at[3, cut], part_in.at[cut], part_ss.at[i], part_rs.at[i], part_peer)
               for i, cut in enumerate([pl.ds(0, early), pl.ds(early, quarter - early)])]
     across[0].start()
@@ -172,10 +173,7 @@
     smem = pl.BlockSpec(memory_space=pltpu.SMEM)
     vmem = pl.BlockSpec(memory_space=pltpu.VMEM)
     dma = pltpu.SemaphoreType.DMA
-    here = lax.axis_index("part")
-    orders = block_order.reshape(PARTS, -1)
-    orders = jnp.where(here == 0, orders[::-1], orders).reshape(-1)
-    sent = order_columns(jacobian, root_weight, orders, PARTS, n)
+    sent = order_columns(jacobian, root_weight, block_order, PARTS, n)
     held_cols = pltpu.VMEM((slots, n * rows, BLOCK), jnp.bfloat16)
     group = (quarter, BLOCK, BLOCK)
     held = pl.pallas_call(

time: 151 us -> 150 us (level)
  no operation moved by 1% of the time
where the time goes in v4:
time: 150 us; the launch traced here: 149 us
  Pallas kernels  144 us (96%)
  other arithmetic  2.34 us (2%)
  local copies, waits for them, and re-layouts  2.2 us (1%)
    pallas_call x1, Pallas kernels, body(): pl.pallas_call(functools.partial(kernel, n, rows, quarter), out_shape=jax...  135 us
    pallas_call x1, Pallas kernels, order_columns(): pl.pallas_call(functools.partial(order_kernel, slots, parts, per_part), o...  8.96 us

profile of v4, /device:TPU:3, one launch (start us, length us, event | category | flops | bytes accessed | tf_op | source)
XLA Modules:
  0.0 148.9 jit_solution(14590162372784292731)
XLA Ops:
  0.0 0.7 sqrt_bitcast_fusion
  0.7 0.1 copy.9.weight_ref
  0.8 0.0 copy-start
  0.8 0.7 copy-done
  1.4 0.0 copy-start.1
  1.4 9.0 %shard_map.55.sent_ref = bf16[4,2,64,64,128]{4,3,2,1,0:T(8,128)(2,1)} custom-call(s32[512]{0:T(512)S(1)} %copy-done, bf16[64,65536]{1,0:T(8,128)(2,1)} %jac_ref.1, f32[64,1]{1,0:T(8,128)S(1)} %copy.9.weight_ref), custom_call_target="tpu_custom_call" | custom-call | tf_op jit(solution)/shard_map/pallas_call | solution.py:33
  10.4 0.0 copy-done.1
  10.4 0.1 copy.8
  10.5 0.7 reshape.8.own_list.own_row
  11.2 134.7 %shard_map.56 = f32[16,128,128]{2,1,0:T(8,128)} custom-call(s32[1,128]{1,0:T(1,128)} %reshape.8.own_list.own_row, s32[1,128]{1,0:T(1,128)} %reshape.8.own_list.own_row, bf16[4,2,64,64,128]{4,3,2,1,0:T(8,128)(2,1)} %shard_map.55.sent_ref), custom_call_target="tpu_custom_call" | custom-call | tf_op jit(solution)/shard_map/pallas_call | solution.py:179
  146.5 2.3 %broadcast_select_fusion = f32[16,128,128]{2,1,0:T(8,128)} fusion(f32[16,128,128]{2,1,0:T(8,128)} %shard_map.56, pred[16]{0:T(512)(128)(4,1)S(1)} %add_compare_fusion), kind=kLoop, calls=%fused_computation | loop fusion | flops 262144 | bytes 2097168 | tf_op jit(solution)/shard_map/jit(_where)/select_n | solution.py:201
  (1 shorter events, 0.0 us)
Async XLA Ops:
  0.8 0.7 copy-start
  1.4 9.0 %copy-start.1 = (s32[1,64,2]{1,2,0:T(2,128)S(1)}, s32[1,64,2]{1,2,0:T(2,128)}, u32[]{:S(2)}) copy-start(s32[1,64,2]{1,2,0:T(2,128)} %param.8) | copy-start | bytes 1540
